TPU v7x, 256 devices: a whole 4x4x8 slice. The times are simulated.
256 devices in a mesh: pipe: 4 (over z_lo, core), fsdp: 64 (over x, z_hi, y).
Axes of the slice: x: 4, y: 4, z: 8 (z_hi: 4, z_lo: 2; z = z_hi * 2 + z_lo), core: 2. Of those that a mesh axis runs over, the one named last changes fastest.
Arguments:
- tokens: int32 [2, 160], replicated, may hold values from 0 to 511
- embed: bfloat16 [512, 8192], P(None, 'fsdp'), may hold values from -60 to 60
- gain: bfloat16 [4, 8192], P('pipe', 'fsdp'), may hold values from 0.099609375 to 1.8984375
- w_in: bfloat16 [4, 3, 8192, 8192], P('pipe', None, None, 'fsdp'), may hold values from -0.0625 to 0.0625
- short_filter: float32 [4, 3, 7, 8192], P('pipe', None, None, 'fsdp'), may hold values from -2 to 2
- long_filter: float32 [4, 512, 128], P('pipe', 'fsdp'), may hold values from -0.5 to 0.5
- skip_bias: float32 [4, 8192], P('pipe', 'fsdp'), may hold values from -1 to 1
- w_out: bfloat16 [4, 8192, 8192], P('pipe', None, 'fsdp'), may hold values from -0.0625 to 0.0625
Outputs:
- hidden: bfloat16 [2, 160, 8192], P(None, 'pipe', 'fsdp')
All inputs are finite; a program needn't handle non-finite values.
Results may differ from a plain program's by a relative error of at most 0.035.
Values may be sent and summed in bfloat16 or wider, within the bound.
No kernel may reach another device: no remote copies, remote signals or barrier semaphores. Data moves between devices by JAX's collectives and lax.ppermute only.
A program may use at most 64 MiB of HBM per device.

v0:
```python
import jax
import jax.numpy as jnp
from jax import lax
from jax.sharding import PartitionSpec as P

D = 8192
GROUP = 16


def from_behind(block, axis, distance):
    devices = range(lax.axis_size(axis))
    route = [(i - distance, i) for i in devices if i - distance in devices]
    return lax.ppermute(block, axis, route)


def spread(value, axis, root):
    mine = lax.axis_index(axis) == root
    return lax.psum(jnp.where(mine, value, jnp.zeros_like(value)), axis)


def short_mix(projected, filters):
    width = filters.shape[1]
    seq_len = projected.shape[1]
    padded = jnp.pad(projected.astype(jnp.float32), ((0, 0), (width - 1, 0), (0, 0)))
    running = jnp.zeros(projected.shape, jnp.float32)
    for offset in range(width):
        window = padded[:, width - 1 - offset : width - 1 - offset + seq_len, :]
        running = running + filters[:, offset][:, None, :] * window
    return running


def long_mix(signal, kernels, group_size):
    seq_len = signal.shape[0]
    span = kernels.shape[1]
    count_filters = kernels.shape[0]
    positions = jnp.arange(seq_len, dtype=jnp.int32)
    lag_table = positions[:, None] - positions[None, :]
    inside = (lag_table >= 0) & (lag_table < span)
    lag_index = jnp.clip(lag_table, 0, span - 1)
    toeplitz = jnp.where(inside[None, :, :], kernels[:, lag_index], jnp.float32(0.0))
    grouped = signal.reshape(seq_len, count_filters, group_size)
    mixed = jnp.einsum("fts,sfg->tfg", toeplitz, grouped, precision=lax.Precision.HIGHEST)
    return mixed.reshape(seq_len, count_filters * group_size)


def body(tokens, embed, gain, w_in, short_filter, long_filter, skip_bias, w_out):
    segment_count = lax.axis_size("pipe")
    segment_index = lax.axis_index("pipe")
    batch_count = tokens.shape[0]
    seq_len = tokens.shape[1]
    local_width = embed.shape[1]
    in_weights = w_in[0]
    short_taps = short_filter[0]
    long_taps = long_filter[0]
    skip_row = skip_bias[0]
    out_weight = w_out[0]
    vocab_index = jnp.arange(embed.shape[0], dtype=jnp.int32)

    def layer_step(activation):
        widened = activation.astype(jnp.float32)
        squares = lax.psum(jnp.sum(widened * widened, axis=1), "fsdp")
        inverse_rms = lax.rsqrt(squares / D + 1e-06)[:, None]
        normalized = (widened * inverse_rms * gain.astype(jnp.float32)).astype(jnp.bfloat16)
        weight_rows = in_weights
        projected = jnp.einsum(
            "sk,jkc->jsc",
            lax.all_gather(normalized, "fsdp", axis=1, tiled=True),
            weight_rows,
            preferred_element_type=jnp.float32,
        )
        mixed = short_mix(projected.astype(jnp.bfloat16), short_taps)
        product = mixed[1] * mixed[2]
        carried = long_mix(product, long_taps, GROUP) + skip_row[None, :] * product
        gated = (mixed[0] * carried).astype(jnp.bfloat16)
        weight_rows = out_weight
        projected_out = jnp.dot(
            lax.all_gather(gated, "fsdp", axis=1, tiled=True),
            weight_rows,
            preferred_element_type=jnp.float32,
        )
        return (widened + projected_out).astype(jnp.bfloat16)

    def tick_body(tick_index, carry_state):
        previous, collected = carry_state
        incoming = from_behind(previous, "pipe", 1)
        micro_index = tick_index - segment_index
        chosen = jnp.clip(micro_index, 0, batch_count - 1)
        token_ids = lax.dynamic_index_in_dim(tokens, chosen, 0, keepdims=False)
        one_hot = (token_ids[:, None] == vocab_index[None, :]).astype(jnp.bfloat16)
        embedded = jnp.dot(one_hot, embed, preferred_element_type=jnp.float32).astype(jnp.bfloat16)
        activation = jnp.where(segment_index == 0, embedded, incoming)
        layer_out = layer_step(activation)
        store_flag = (
            (micro_index >= 0) & (micro_index < batch_count) & (segment_index == segment_count - 1)
        )
        updated = lax.dynamic_update_index_in_dim(collected, layer_out, chosen, 0)
        collected = jnp.where(store_flag, updated, collected)
        return (layer_out, collected)

    start_state = (
        jnp.zeros((seq_len, local_width), jnp.bfloat16),
        jnp.zeros((batch_count, seq_len, local_width), jnp.bfloat16),
    )
    final_state = lax.fori_loop(0, batch_count + segment_count - 1, tick_body, start_state)
    finished = spread(final_state[1], "pipe", segment_count - 1)
    row_share = seq_len // segment_count
    return lax.dynamic_slice_in_dim(finished, segment_index * row_share, row_share, 1)


def solution(mesh):
    return jax.shard_map(
        body,
        mesh=mesh,
        in_specs=(
            P(),
            P(None, "fsdp"),
            P("pipe", "fsdp"),
            P("pipe", None, None, "fsdp"),
            P("pipe", None, None, "fsdp"),
            P("pipe", "fsdp", None),
            P("pipe", "fsdp"),
            P("pipe", None, "fsdp"),
        ),
        out_specs=P(None, "pipe", "fsdp"),
        check_vma=False,
    )
```

profile of v0, /device:TPU:1, one launch (start us, length us, event | category | flops | bytes accessed | tf_op | source)
XLA Modules:
  0.0 2043.1 jit_solution(8263287136697875596)
XLA Ops:
  10.1 1982.0 %while.18 = (s32[]{:T(128)}, bf16[160,128]{1,0:T(8,128)(2,1)}, bf16[2,160,128]{2,1,0:T(8,128)(2,1)}, pred[]{:T(512)}, s32[]{:T(128)}, /*index=5*/s32[2,160]{1,0:...) while((s32[]{:T(128)}, bf16[160,128]{1,0:T(8,128)(2,1)}, ...), condition=%wide.region_3.4_spmd.clone, body=%wide.region_0.3_spmd.clone.sunk | while | flops 1404303872 | bytes 46493152 | solution.py:104
  17.7 168.4 %psum.24 = f32[160]{0:T(256)S(1)} all-reduce(f32[160]{0:T(256)S(1)} %get-tuple-element.508), channel_id=1, replica_groups=mesh['pipe'=4,'fsdp'=64] {'fsdp'}, use_global_device_ids=true, to_apply=%region_2.2 | all-reduce | flops 160 | bytes 1280 | tf_op jit(solution)/shard_map/while/body/eval_jaxpr/psum | solution.py:61
  187.1 85.3 %gather_fusion = f32[25600,8]{1,0:T(8,128)} fusion(f32[8,128]{0,1:T(8,128)S(1)} %get-tuple-element.562, s32[25600]{0:T(1024)S(1)} %broadcast_clamp_fusion.2), kind=kCustom, calls=%fused_computation.clone.clone.1 | custom fusion | bytes 1740800 | tf_op jit(solution)/shard_map/while/body/eval_jaxpr/gather | solution.py:40
  283.2 13.5 all-gather.3.cloned.1.call-done
  310.4 96.4 %all-gather.5.cloned.1.call-done = bf16[160,8192]{1,0:T(8,128)(2,1)} async-done(((bf16[160,128]{1,0:T(8,128)(2,1)}), bf16[160,8192]{1,0:T(8,128)(2,1)}) %all-gather.5.cloned.1.call-update) | async-done | bytes 2621456 | tf_op jit(solution)/shard_map/while/body/eval_jaxpr/all_gather | solution.py:77
  415.4 166.0 %psum.24 = f32[160]{0:T(256)S(1)} all-reduce(f32[160]{0:T(256)S(1)} %get-tuple-element.508), channel_id=1, replica_groups=mesh['pipe'=4,'fsdp'=64] {'fsdp'}, use_global_device_ids=true, to_apply=%region_2.2 | all-reduce | flops 160 | bytes 1280 | tf_op jit(solution)/shard_map/while/body/eval_jaxpr/psum | solution.py:61
  582.4 85.3 %gather_fusion = f32[25600,8]{1,0:T(8,128)} fusion(f32[8,128]{0,1:T(8,128)S(1)} %get-tuple-element.562, s32[25600]{0:T(1024)S(1)} %broadcast_clamp_fusion.2), kind=kCustom, calls=%fused_computation.clone.clone.1 | custom fusion | bytes 1740800 | tf_op jit(solution)/shard_map/while/body/eval_jaxpr/gather | solution.py:40
  678.5 13.8 all-gather.3.cloned.1.call-done
  706.1 96.3 %all-gather.5.cloned.1.call-done = bf16[160,8192]{1,0:T(8,128)(2,1)} async-done(((bf16[160,128]{1,0:T(8,128)(2,1)}), bf16[160,8192]{1,0:T(8,128)(2,1)}) %all-gather.5.cloned.1.call-update) | async-done | bytes 2621456 | tf_op jit(solution)/shard_map/while/body/eval_jaxpr/all_gather | solution.py:77
  810.9 166.0 %psum.24 = f32[160]{0:T(256)S(1)} all-reduce(f32[160]{0:T(256)S(1)} %get-tuple-element.508), channel_id=1, replica_groups=mesh['pipe'=4,'fsdp'=64] {'fsdp'}, use_global_device_ids=true, to_apply=%region_2.2 | all-reduce | flops 160 | bytes 1280 | tf_op jit(solution)/shard_map/while/body/eval_jaxpr/psum | solution.py:61
  977.9 85.3 %gather_fusion = f32[25600,8]{1,0:T(8,128)} fusion(f32[8,128]{0,1:T(8,128)S(1)} %get-tuple-element.562, s32[25600]{0:T(1024)S(1)} %broadcast_clamp_fusion.2), kind=kCustom, calls=%fused_computation.clone.clone.1 | custom fusion | bytes 1740800 | tf_op jit(solution)/shard_map/while/body/eval_jaxpr/gather | solution.py:40
  1063.1 8.8 copy.25
  1074.0 13.8 all-gather.3.cloned.1.call-done
  1101.6 96.3 %all-gather.5.cloned.1.call-done = bf16[160,8192]{1,0:T(8,128)(2,1)} async-done(((bf16[160,128]{1,0:T(8,128)(2,1)}), bf16[160,8192]{1,0:T(8,128)(2,1)}) %all-gather.5.cloned.1.call-update) | async-done | bytes 2621456 | tf_op jit(solution)/shard_map/while/body/eval_jaxpr/all_gather | solution.py:77
  1206.4 166.0 %psum.24 = f32[160]{0:T(256)S(1)} all-reduce(f32[160]{0:T(256)S(1)} %get-tuple-element.508), channel_id=1, replica_groups=mesh['pipe'=4,'fsdp'=64] {'fsdp'}, use_global_device_ids=true, to_apply=%region_2.2 | all-reduce | flops 160 | bytes 1280 | tf_op jit(solution)/shard_map/while/body/eval_jaxpr/psum | solution.py:61
  1373.4 85.3 %gather_fusion = f32[25600,8]{1,0:T(8,128)} fusion(f32[8,128]{0,1:T(8,128)S(1)} %get-tuple-element.562, s32[25600]{0:T(1024)S(1)} %broadcast_clamp_fusion.2), kind=kCustom, calls=%fused_computation.clone.clone.1 | custom fusion | bytes 1740800 | tf_op jit(solution)/shard_map/while/body/eval_jaxpr/gather | solution.py:40
  1458.6 8.8 copy.25
  1469.5 13.8 all-gather.3.cloned.1.call-done
  1497.1 96.3 %all-gather.5.cloned.1.call-done = bf16[160,8192]{1,0:T(8,128)(2,1)} async-done(((bf16[160,128]{1,0:T(8,128)(2,1)}), bf16[160,8192]{1,0:T(8,128)(2,1)}) %all-gather.5.cloned.1.call-update) | async-done | bytes 2621456 | tf_op jit(solution)/shard_map/while/body/eval_jaxpr/all_gather | solution.py:77
  1601.9 166.0 %psum.24 = f32[160]{0:T(256)S(1)} all-reduce(f32[160]{0:T(256)S(1)} %get-tuple-element.508), channel_id=1, replica_groups=mesh['pipe'=4,'fsdp'=64] {'fsdp'}, use_global_device_ids=true, to_apply=%region_2.2 | all-reduce | flops 160 | bytes 1280 | tf_op jit(solution)/shard_map/while/body/eval_jaxpr/psum | solution.py:61
  1768.9 85.3 %gather_fusion = f32[25600,8]{1,0:T(8,128)} fusion(f32[8,128]{0,1:T(8,128)S(1)} %get-tuple-element.562, s32[25600]{0:T(1024)S(1)} %broadcast_clamp_fusion.2), kind=kCustom, calls=%fused_computation.clone.clone.1 | custom fusion | bytes 1740800 | tf_op jit(solution)/shard_map/while/body/eval_jaxpr/gather | solution.py:40
  1865.0 13.8 all-gather.3.cloned.1.call-done
  1892.6 96.3 %all-gather.5.cloned.1.call-done = bf16[160,8192]{1,0:T(8,128)(2,1)} async-done(((bf16[160,128]{1,0:T(8,128)(2,1)}), bf16[160,8192]{1,0:T(8,128)(2,1)}) %all-gather.5.cloned.1.call-update) | async-done | bytes 2621456 | tf_op jit(solution)/shard_map/while/body/eval_jaxpr/all_gather | solution.py:77
  1992.7 41.6 %all-reduce.3.cloned.1.call-done = bf16[2,160,128]{2,1,0:T(8,128)(2,1)} async-done(((bf16[2,160,128]{2,1,0:T(8,128)(2,1)}), bf16[2,160,128]{2,1,0:T(8,128)(2,1)}) %all-reduce.3.cloned.1.call-update) | async-done | bytes 81936 | tf_op jit(solution)/shard_map/psum | solution.py:18
  (226 shorter events, 159.2 us)
Async XLA Ops:
  10.1 286.6 %all-gather.3.cloned.1.call-start = ((), (), s32[]{:S(2)}) async-start(), calls=%async_computation.1 | async-start | bytes 2662400 | tf_op jit(solution)/shard_map/while/body/eval_jaxpr/all_gather | solution.py:67
  10.1 6.3 collective-permute-start
  186.8 220.0 %all-gather.5.cloned.1.call-start = ((), (), s32[]{:S(2)}) async-start(), calls=%async_computation.2 | async-start | bytes 2662400 | tf_op jit(solution)/shard_map/while/body/eval_jaxpr/all_gather | solution.py:77
  301.8 105.1 %copy-start = (bf16[8192,128]{1,0:T(8,128)(2,1)S(1)}, bf16[8192,128]{1,0:T(8,128)(2,1)}, u32[]{:S(2)}) copy-start(bf16[8192,128]{1,0:T(8,128)(2,1)} %get-tuple-element.564) | copy-start | bytes 6291460 | tf_op jit(solution)/shard_map/while
  410.1 282.2 %all-gather.3.cloned.1.call-start = ((), (), s32[]{:S(2)}) async-start(), calls=%async_computation.1 | async-start | bytes 2662400 | tf_op jit(solution)/shard_map/while/body/eval_jaxpr/all_gather | solution.py:67
  410.9 3.3 collective-permute-start
  582.1 220.2 %all-gather.5.cloned.1.call-start = ((), (), s32[]{:S(2)}) async-start(), calls=%async_computation.2 | async-start | bytes 2662400 | tf_op jit(solution)/shard_map/while/body/eval_jaxpr/all_gather | solution.py:77
  692.3 5.2 copy-start.7
  692.3 5.2 copy-start.8
  697.4 104.9 %copy-start = (bf16[8192,128]{1,0:T(8,128)(2,1)S(1)}, bf16[8192,128]{1,0:T(8,128)(2,1)}, u32[]{:S(2)}) copy-start(bf16[8192,128]{1,0:T(8,128)(2,1)} %get-tuple-element.564) | copy-start | bytes 6291460 | tf_op jit(solution)/shard_map/while
  805.6 282.2 %all-gather.3.cloned.1.call-start = ((), (), s32[]{:S(2)}) async-start(), calls=%async_computation.1 | async-start | bytes 2662400 | tf_op jit(solution)/shard_map/while/body/eval_jaxpr/all_gather | solution.py:67
  806.4 3.3 collective-permute-start
  977.6 220.2 %all-gather.5.cloned.1.call-start = ((), (), s32[]{:S(2)}) async-start(), calls=%async_computation.2 | async-start | bytes 2662400 | tf_op jit(solution)/shard_map/while/body/eval_jaxpr/all_gather | solution.py:77
  1087.8 5.2 copy-start.7
  1093.0 104.9 %copy-start = (bf16[8192,128]{1,0:T(8,128)(2,1)S(1)}, bf16[8192,128]{1,0:T(8,128)(2,1)}, u32[]{:S(2)}) copy-start(bf16[8192,128]{1,0:T(8,128)(2,1)} %get-tuple-element.564) | copy-start | bytes 6291460 | tf_op jit(solution)/shard_map/while
  1201.1 282.2 %all-gather.3.cloned.1.call-start = ((), (), s32[]{:S(2)}) async-start(), calls=%async_computation.1 | async-start | bytes 2662400 | tf_op jit(solution)/shard_map/while/body/eval_jaxpr/all_gather | solution.py:67
  1201.9 3.3 collective-permute-start
  1373.1 220.2 %all-gather.5.cloned.1.call-start = ((), (), s32[]{:S(2)}) async-start(), calls=%async_computation.2 | async-start | bytes 2662400 | tf_op jit(solution)/shard_map/while/body/eval_jaxpr/all_gather | solution.py:77
  1488.4 104.9 %copy-start = (bf16[8192,128]{1,0:T(8,128)(2,1)S(1)}, bf16[8192,128]{1,0:T(8,128)(2,1)}, u32[]{:S(2)}) copy-start(bf16[8192,128]{1,0:T(8,128)(2,1)} %get-tuple-element.564) | copy-start | bytes 6291460 | tf_op jit(solution)/shard_map/while
  1596.6 282.2 %all-gather.3.cloned.1.call-start = ((), (), s32[]{:S(2)}) async-start(), calls=%async_computation.1 | async-start | bytes 2662400 | tf_op jit(solution)/shard_map/while/body/eval_jaxpr/all_gather | solution.py:67
  1597.4 3.3 collective-permute-start
  1768.6 220.2 %all-gather.5.cloned.1.call-start = ((), (), s32[]{:S(2)}) async-start(), calls=%async_computation.2 | async-start | bytes 2662400 | tf_op jit(solution)/shard_map/while/body/eval_jaxpr/all_gather | solution.py:77
  1883.9 104.9 %copy-start = (bf16[8192,128]{1,0:T(8,128)(2,1)S(1)}, bf16[8192,128]{1,0:T(8,128)(2,1)}, u32[]{:S(2)}) copy-start(bf16[8192,128]{1,0:T(8,128)(2,1)} %get-tuple-element.564) | copy-start | bytes 6291460 | tf_op jit(solution)/shard_map/while
  1992.1 42.3 %all-reduce.3.cloned.1.call-start = ((), (), s32[]{:S(2)}) async-start(), calls=%async_computation | async-start | bytes 163840 | tf_op jit(solution)/shard_map/psum | solution.py:18
  (37 other events, 169.1 us)
Sparse Core Ops, SparseCore 0:
  187.0 109.6 all-gather.2
  310.6 96.2 all-gather.4
  582.2 110.0 all-gather.2
  706.2 96.1 all-gather.4
  977.7 110.0 all-gather.2
  1101.7 96.1 all-gather.4
  1373.2 110.0 all-gather.2
  1497.2 96.1 all-gather.4
  1768.7 110.0 all-gather.2
  1892.7 96.1 all-gather.4
Sparse Core Ops, SparseCore 1:
  1995.2 39.2 all-reduce.2
where the time goes:
time: 2050 us; the launch traced here: 2040 us
  blocking collectives  832 us (41%)
  waiting for transfers between devices  592 us (29%)
  local copies, waits for them, and re-layouts  502 us (24%)
  matrix products  61.6 us (3%)
  other arithmetic  26.4 us (1%)
    psum x5, blocking collectives, layer_step(): squares = lax.psum(jnp.sum(widened * widened, axis=1), 'fsdp')  832 us
    all_gather x5, waiting for transfers between devices, layer_step(): lax.all_gather(gated, 'fsdp', axis=1, tiled=True)  482 us
    gather x10, local copies, waits for them, and re-layouts, long_mix(): kernels[:, lag_index]  470 us
    all_gather x5, waiting for transfers between devices, layer_step(): lax.all_gather(normalized, 'fsdp', axis=1, tiled=True)  68.8 us
    psum x1, waiting for transfers between devices, spread(): return lax.psum(jnp.where(mine, value, jnp.zeros_like(value)), axis)  41.6 us
  transfers between devices with their start and end apart: 16, of which 11 were waited for; matrix products, arithmetic and copies ran while one was open for 24% of the time, Pallas kernels for 0%

commit v1 on v0

--- a/solution.py
+++ b/solution.py
@@ -64,7 +64,10 @@
         weight_rows = in_weights
         projected = jnp.einsum(
             "sk,jkc->jsc",
-            lax.all_gather(normalized, "fsdp", axis=1, tiled=True),
+            jnp.concatenate(
+                lax.all_to_all(jnp.stack([normalized] * lax.axis_size("fsdp")), "fsdp", 0, 0),
+                axis=1,
+            ),
             weight_rows,
             preferred_element_type=jnp.float32,
         )

time: 2050 us -> 2210 us (1.078)
  waiting for transfers between devices: 592 us -> 683 us
  local copies, waits for them, and re-layouts: 502 us -> 553 us
  starting transfers between devices: 12.8 us -> 36.4 us
    all_gather x5, waiting for transfers between devices: 482 us -> 641 us  [layer_step(): lax.all_gather(gated, 'fsdp', axis=1, tiled=True)]
    all_gather x5 -> x0, waiting for transfers between devices: 68.8 us -> none  [layer_step(): lax.all_gather(normalized, 'fsdp', axis=1, tiled=True)]
    reshape x0 -> x10, local copies, waits for them, and re-layouts: none -> 38.5 us  [layer_step(): jnp.concatenate(lax.all_to_all(jnp.stack([normalized] * lax.axis_size('fs...]
    all_to_all x0 -> x5, starting transfers between devices: none -> 23.6 us  [layer_step(): lax.all_to_all(jnp.stack([normalized] * lax.axis_size('fsdp')), 'fsdp', 0...]
  transfers between devices with their start and end apart: 16 -> 16, of which waited for: 11 -> 6; matrix products, arithmetic and copies ran while one was open for 24% -> 22% of each run, Pallas kernels for 0% -> 0%
where the time goes in v1:
time: 2210 us; the launch traced here: 2200 us
  blocking collectives  832 us (38%)
  waiting for transfers between devices  683 us (31%)
  local copies, waits for them, and re-layouts  553 us (25%)
  matrix products  61.9 us (3%)
  starting transfers between devices  36.4 us (2%)
    psum x5, blocking collectives, layer_step(): squares = lax.psum(jnp.sum(widened * widened, axis=1), 'fsdp')  832 us
    all_gather x5, waiting for transfers between devices, layer_step(): lax.all_gather(gated, 'fsdp', axis=1, tiled=True)  641 us
    gather x10, local copies, waits for them, and re-layouts, long_mix(): kernels[:, lag_index]  474 us
  transfers between devices with their start and end apart: 16, of which 6 were waited for; matrix products, arithmetic and copies ran while one was open for 22% of the time, Pallas kernels for 0%

profile of v1, /device:TPU:1, one launch (start us, length us, event | category | flops | bytes accessed | tf_op | source)
XLA Modules:
  0.0 2202.6 jit_solution(6869731706732440427)
XLA Ops:
  10.1 2141.7 %while.18 = (s32[]{:T(128)}, bf16[160,128]{1,0:T(8,128)(2,1)S(1)}, bf16[2,160,128]{2,1,0:T(8,128)(2,1)}, pred[]{:T(512)}, s32[]{:T(128)}, /*index=5*/s32[2,160]{...) while((s32[]{:T(128)}, bf16[160,128]{1,0:T(8,128)(2,1)S(1)}, ...), condition=%wide.region_3.4_spmd.clone, body=%wide.region_0.3_spmd.clone.sunk | while | flops 1404303872 | bytes 62795252 | solution.py:107
  17.7 168.4 %psum.24 = f32[160]{0:T(256)S(1)} all-reduce(f32[160]{0:T(256)S(1)} %get-tuple-element.508), channel_id=1, replica_groups=mesh['pipe'=4,'fsdp'=64] {'fsdp'}, use_global_device_ids=true, to_apply=%region_2.2 | all-reduce | flops 160 | bytes 1280 | tf_op jit(solution)/shard_map/while/body/eval_jaxpr/psum | solution.py:61
  193.0 85.3 %gather_fusion = f32[25600,8]{1,0:T(8,128)} fusion(f32[8,128]{0,1:T(8,128)S(1)} %get-tuple-element.562, s32[25600]{0:T(1024)S(1)} %broadcast_clamp_fusion.2), kind=kCustom, calls=%fused_computation.clone.clone.1 | custom fusion | bytes 1740800 | tf_op jit(solution)/shard_map/while/body/eval_jaxpr/gather | solution.py:40
  278.2 9.5 copy.33
  297.5 5.2 fusion.48
  311.4 123.9 %all-gather.2.cloned.1.call-done = bf16[160,8192]{1,0:T(8,128)(2,1)} async-done(((bf16[160,128]{1,0:T(8,128)(2,1)}), bf16[160,8192]{1,0:T(8,128)(2,1)}) %all-gather.2.cloned.1.call-update) | async-done | bytes 2621456 | tf_op jit(solution)/shard_map/while/body/eval_jaxpr/all_gather | solution.py:80
  443.0 166.0 %psum.24 = f32[160]{0:T(256)S(1)} all-reduce(f32[160]{0:T(256)S(1)} %get-tuple-element.508), channel_id=1, replica_groups=mesh['pipe'=4,'fsdp'=64] {'fsdp'}, use_global_device_ids=true, to_apply=%region_2.2 | all-reduce | flops 160 | bytes 1280 | tf_op jit(solution)/shard_map/while/body/eval_jaxpr/psum | solution.py:61
  615.8 85.3 %gather_fusion = f32[25600,8]{1,0:T(8,128)} fusion(f32[8,128]{0,1:T(8,128)S(1)} %get-tuple-element.562, s32[25600]{0:T(1024)S(1)} %broadcast_clamp_fusion.2), kind=kCustom, calls=%fused_computation.clone.clone.1 | custom fusion | bytes 1740800 | tf_op jit(solution)/shard_map/while/body/eval_jaxpr/gather | solution.py:40
  701.1 9.5 copy.33
  720.4 5.2 fusion.48
  734.3 129.4 %all-gather.2.cloned.1.call-done = bf16[160,8192]{1,0:T(8,128)(2,1)} async-done(((bf16[160,128]{1,0:T(8,128)(2,1)}), bf16[160,8192]{1,0:T(8,128)(2,1)}) %all-gather.2.cloned.1.call-update) | async-done | bytes 2621456 | tf_op jit(solution)/shard_map/while/body/eval_jaxpr/all_gather | solution.py:80
  871.5 166.0 %psum.24 = f32[160]{0:T(256)S(1)} all-reduce(f32[160]{0:T(256)S(1)} %get-tuple-element.508), channel_id=1, replica_groups=mesh['pipe'=4,'fsdp'=64] {'fsdp'}, use_global_device_ids=true, to_apply=%region_2.2 | all-reduce | flops 160 | bytes 1280 | tf_op jit(solution)/shard_map/while/body/eval_jaxpr/psum | solution.py:61
  1044.3 85.3 %gather_fusion = f32[25600,8]{1,0:T(8,128)} fusion(f32[8,128]{0,1:T(8,128)S(1)} %get-tuple-element.562, s32[25600]{0:T(1024)S(1)} %broadcast_clamp_fusion.2), kind=kCustom, calls=%fused_computation.clone.clone.1 | custom fusion | bytes 1740800 | tf_op jit(solution)/shard_map/while/body/eval_jaxpr/gather | solution.py:40
  1129.6 9.5 copy.33
  1162.7 129.0 %all-gather.2.cloned.1.call-done = bf16[160,8192]{1,0:T(8,128)(2,1)} async-done(((bf16[160,128]{1,0:T(8,128)(2,1)}), bf16[160,8192]{1,0:T(8,128)(2,1)}) %all-gather.2.cloned.1.call-update) | async-done | bytes 2621456 | tf_op jit(solution)/shard_map/while/body/eval_jaxpr/all_gather | solution.py:80
  1299.5 166.0 %psum.24 = f32[160]{0:T(256)S(1)} all-reduce(f32[160]{0:T(256)S(1)} %get-tuple-element.508), channel_id=1, replica_groups=mesh['pipe'=4,'fsdp'=64] {'fsdp'}, use_global_device_ids=true, to_apply=%region_2.2 | all-reduce | flops 160 | bytes 1280 | tf_op jit(solution)/shard_map/while/body/eval_jaxpr/psum | solution.py:61
  1472.3 85.3 %gather_fusion = f32[25600,8]{1,0:T(8,128)} fusion(f32[8,128]{0,1:T(8,128)S(1)} %get-tuple-element.562, s32[25600]{0:T(1024)S(1)} %broadcast_clamp_fusion.2), kind=kCustom, calls=%fused_computation.clone.clone.1 | custom fusion | bytes 1740800 | tf_op jit(solution)/shard_map/while/body/eval_jaxpr/gather | solution.py:40
  1557.6 9.5 copy.33
  1590.7 129.4 %all-gather.2.cloned.1.call-done = bf16[160,8192]{1,0:T(8,128)(2,1)} async-done(((bf16[160,128]{1,0:T(8,128)(2,1)}), bf16[160,8192]{1,0:T(8,128)(2,1)}) %all-gather.2.cloned.1.call-update) | async-done | bytes 2621456 | tf_op jit(solution)/shard_map/while/body/eval_jaxpr/all_gather | solution.py:80
  1727.9 166.0 %psum.24 = f32[160]{0:T(256)S(1)} all-reduce(f32[160]{0:T(256)S(1)} %get-tuple-element.508), channel_id=1, replica_groups=mesh['pipe'=4,'fsdp'=64] {'fsdp'}, use_global_device_ids=true, to_apply=%region_2.2 | all-reduce | flops 160 | bytes 1280 | tf_op jit(solution)/shard_map/while/body/eval_jaxpr/psum | solution.py:61
  1900.8 85.3 %gather_fusion = f32[25600,8]{1,0:T(8,128)} fusion(f32[8,128]{0,1:T(8,128)S(1)} %get-tuple-element.562, s32[25600]{0:T(1024)S(1)} %broadcast_clamp_fusion.2), kind=kCustom, calls=%fused_computation.clone.clone.1 | custom fusion | bytes 1740800 | tf_op jit(solution)/shard_map/while/body/eval_jaxpr/gather | solution.py:40
  1986.0 9.5 copy.33
  2019.2 129.4 %all-gather.2.cloned.1.call-done = bf16[160,8192]{1,0:T(8,128)(2,1)} async-done(((bf16[160,128]{1,0:T(8,128)(2,1)}), bf16[160,8192]{1,0:T(8,128)(2,1)}) %all-gather.2.cloned.1.call-update) | async-done | bytes 2621456 | tf_op jit(solution)/shard_map/while/body/eval_jaxpr/all_gather | solution.py:80
  2152.5 41.6 %all-reduce.3.cloned.1.call-done = bf16[2,160,128]{2,1,0:T(8,128)(2,1)} async-done(((bf16[2,160,128]{2,1,0:T(8,128)(2,1)}), bf16[2,160,128]{2,1,0:T(8,128)(2,1)}) %all-reduce.3.cloned.1.call-update) | async-done | bytes 81936 | tf_op jit(solution)/shard_map/psum | solution.py:18
  (246 shorter events, 187.6 us)
Async XLA Ops:
  10.1 6.3 collective-permute-start
  188.0 101.8 %all-to-all-start = ((bf16[64,160,128]{2,1,0:T(8,128)(2,1)}), bf16[64,160,128]{2,1,0:T(8,128)(2,1)S(1)}, u32[]{:S(2)}, u32[]{:S(2)}) async-start(bf16[64,160,128]{2,1,0:T(8,128)(2,1)} %stack.8), calls=%async_computation | async-start | bytes 5242880 | tf_op jit(solution)/shard_map/while/body/eval_jaxpr/all_to_all | solution.py:68
  192.7 242.5 %all-gather.2.cloned.1.call-start = ((), (), s32[]{:S(2)}) async-start(), calls=%async_computation.2 | async-start | bytes 2662400 | tf_op jit(solution)/shard_map/while/body/eval_jaxpr/all_gather | solution.py:80
  297.5 8.5 copy-start
  302.7 132.5 %copy-start.1 = (bf16[8192,128]{1,0:T(8,128)(2,1)S(1)}, bf16[8192,128]{1,0:T(8,128)(2,1)}, u32[]{:S(2)}) copy-start(bf16[8192,128]{1,0:T(8,128)(2,1)} %get-tuple-element.564) | copy-start | bytes 6291460 | tf_op jit(solution)/shard_map/while
  438.5 3.3 collective-permute-start
  610.9 101.8 %all-to-all-start = ((bf16[64,160,128]{2,1,0:T(8,128)(2,1)}), bf16[64,160,128]{2,1,0:T(8,128)(2,1)S(1)}, u32[]{:S(2)}, u32[]{:S(2)}) async-start(bf16[64,160,128]{2,1,0:T(8,128)(2,1)} %stack.8), calls=%async_computation | async-start | bytes 5242880 | tf_op jit(solution)/shard_map/while/body/eval_jaxpr/all_to_all | solution.py:68
  615.6 248.1 %all-gather.2.cloned.1.call-start = ((), (), s32[]{:S(2)}) async-start(), calls=%async_computation.2 | async-start | bytes 2662400 | tf_op jit(solution)/shard_map/while/body/eval_jaxpr/all_gather | solution.py:80
  720.4 8.5 copy-start
  725.6 138.1 %copy-start.1 = (bf16[8192,128]{1,0:T(8,128)(2,1)S(1)}, bf16[8192,128]{1,0:T(8,128)(2,1)}, u32[]{:S(2)}) copy-start(bf16[8192,128]{1,0:T(8,128)(2,1)} %get-tuple-element.564) | copy-start | bytes 6291460 | tf_op jit(solution)/shard_map/while
  866.9 3.3 collective-permute-start
  1039.3 101.8 %all-to-all-start = ((bf16[64,160,128]{2,1,0:T(8,128)(2,1)}), bf16[64,160,128]{2,1,0:T(8,128)(2,1)S(1)}, u32[]{:S(2)}, u32[]{:S(2)}) async-start(bf16[64,160,128]{2,1,0:T(8,128)(2,1)} %stack.8), calls=%async_computation | async-start | bytes 5242880 | tf_op jit(solution)/shard_map/while/body/eval_jaxpr/all_to_all | solution.py:68
  1044.1 247.7 %all-gather.2.cloned.1.call-start = ((), (), s32[]{:S(2)}) async-start(), calls=%async_computation.2 | async-start | bytes 2662400 | tf_op jit(solution)/shard_map/while/body/eval_jaxpr/all_gather | solution.py:80
  1148.9 8.5 copy-start
  1154.1 137.6 %copy-start.1 = (bf16[8192,128]{1,0:T(8,128)(2,1)S(1)}, bf16[8192,128]{1,0:T(8,128)(2,1)}, u32[]{:S(2)}) copy-start(bf16[8192,128]{1,0:T(8,128)(2,1)} %get-tuple-element.564) | copy-start | bytes 6291460 | tf_op jit(solution)/shard_map/while
  1294.9 3.3 collective-permute-start
  1467.3 101.8 %all-to-all-start = ((bf16[64,160,128]{2,1,0:T(8,128)(2,1)}), bf16[64,160,128]{2,1,0:T(8,128)(2,1)S(1)}, u32[]{:S(2)}, u32[]{:S(2)}) async-start(bf16[64,160,128]{2,1,0:T(8,128)(2,1)} %stack.8), calls=%async_computation | async-start | bytes 5242880 | tf_op jit(solution)/shard_map/while/body/eval_jaxpr/all_to_all | solution.py:68
  1472.1 248.1 %all-gather.2.cloned.1.call-start = ((), (), s32[]{:S(2)}) async-start(), calls=%async_computation.2 | async-start | bytes 2662400 | tf_op jit(solution)/shard_map/while/body/eval_jaxpr/all_gather | solution.py:80
  1582.1 138.1 %copy-start.1 = (bf16[8192,128]{1,0:T(8,128)(2,1)S(1)}, bf16[8192,128]{1,0:T(8,128)(2,1)}, u32[]{:S(2)}) copy-start(bf16[8192,128]{1,0:T(8,128)(2,1)} %get-tuple-element.564) | copy-start | bytes 6291460 | tf_op jit(solution)/shard_map/while
  1723.4 3.3 collective-permute-start
  1895.8 101.8 %all-to-all-start = ((bf16[64,160,128]{2,1,0:T(8,128)(2,1)}), bf16[64,160,128]{2,1,0:T(8,128)(2,1)S(1)}, u32[]{:S(2)}, u32[]{:S(2)}) async-start(bf16[64,160,128]{2,1,0:T(8,128)(2,1)} %stack.8), calls=%async_computation | async-start | bytes 5242880 | tf_op jit(solution)/shard_map/while/body/eval_jaxpr/all_to_all | solution.py:68
  1900.5 248.1 %all-gather.2.cloned.1.call-start = ((), (), s32[]{:S(2)}) async-start(), calls=%async_computation.2 | async-start | bytes 2662400 | tf_op jit(solution)/shard_map/while/body/eval_jaxpr/all_gather | solution.py:80
  2010.6 138.1 %copy-start.1 = (bf16[8192,128]{1,0:T(8,128)(2,1)S(1)}, bf16[8192,128]{1,0:T(8,128)(2,1)}, u32[]{:S(2)}) copy-start(bf16[8192,128]{1,0:T(8,128)(2,1)} %get-tuple-element.564) | copy-start | bytes 6291460 | tf_op jit(solution)/shard_map/while
  2151.8 42.3 %all-reduce.3.cloned.1.call-start = ((), (), s32[]{:S(2)}) async-start(), calls=%async_computation.1 | async-start | bytes 163840 | tf_op jit(solution)/shard_map/psum | solution.py:18
  (42 other events, 205.3 us)
Sparse Core Ops, SparseCore 0:
  311.5 123.7 all-gather.1
  734.4 129.2 all-gather.1
  1162.8 128.8 all-gather.1
  1590.8 129.2 all-gather.1
  2019.3 129.2 all-gather.1
Sparse Core Ops, SparseCore 1:
  2154.9 39.2 all-reduce.2
